TPU v7x, 32 devices: a whole 2x2x4 slice. The times are simulated.
32 devices in a mesh: bis: 4 (over x, core), slab: 8 (over z, y).
Axes of the slice: x: 2, y: 2, z: 4, core: 2. Of those that a mesh axis runs over, the one named last changes fastest.
Arguments:
- positions: float32 [3, 32, 32768], P(None, None, ('bis', 'slab')), may hold values from 0 to 1
- forces: float32 [3, 32, 32768], P(None, None, ('bis', 'slab')), may hold values from -6 to 6
- self_blocks: bfloat16 [96, 96, 32768], P(None, None, ('bis', 'slab')), may hold values from -0.625 to 0.625
- cut_lists: int32 [3, 8192], P(None, ('bis', 'slab')), may hold values from 0 to 1023, as said below
- pair_tiles: int32 [4, 8192], P(None, ('bis', 'slab')), may hold values from -1 to 8191, as said below
Outputs:
- velocity: float32 [3, 32, 32768], P(None, None, ('bis', 'slab'))
Inputs may be any that keep to these rules, and one draw needn't show every extreme that they name: `cut_lists`: for each level and device the 256 entries are distinct slots of that device. `pair_tiles`: tile id (b * 8 + s) * 256 + t is tile t of device (b, s). Every entry of a device's targets is -1 or a tile of the device with the same slab index and a bis index one lower, equal or one higher, cyclically; each device's entries name exactly 64 distinct tiles of each of its two neighbouring devices.
All inputs are finite; a program needn't handle non-finite values.
Results may differ from a plain program's by a relative error of at most 0.0003.
Values sent between devices are 32-bit elements; how exact they have to be, the bound alone decides.
A program may use at most 128 MiB of HBM per device.

v0:
```python
import math

import jax
import jax.numpy as jnp
from jax import lax
from jax.sharding import PartitionSpec as P

NODES = 32
TILE = 4


blob_eps2 = 0.0025
stokes_scale = 1.0 / (8.0 * math.pi)


def swapped(block, axis, distance):
    count = lax.axis_size(axis)
    route = []
    for low in range(count):
        high = low | 1 << distance
        if high != low and high < count:
            route += [(low, high), (high, low)]
    return lax.ppermute(block, axis, route)


def with_halo(block, sides, width):
    for axis, dim in sides:
        count = lax.axis_size(axis)
        forward = [(i, i + 1) for i in range(count - 1)]
        forward.append((count - 1, 0))
        backward = [(target, source) for source, target in forward]
        low = lax.ppermute(
            lax.slice_in_dim(block, block.shape[dim] - width, None, axis=dim), axis, forward
        )
        high = lax.ppermute(lax.slice_in_dim(block, 0, width, axis=dim), axis, backward)
        block = jnp.concatenate([low, block, high], axis=dim)
    return block


def stokeslet(targets, sources, pushes, weights):
    offset_vec = targets[:, None, :, :, None] - sources[:, :, :, None, :]
    radius2 = jnp.sum(offset_vec * offset_vec, axis=0) + blob_eps2
    inverse = lax.rsqrt(radius2) * weights[:, :, None, None]
    inverse3 = inverse * inverse * inverse
    dot_force = jnp.sum(offset_vec * pushes[:, :, :, None, :], axis=0)
    summed = jnp.sum(
        pushes[:, :, :, None, :] * inverse[None] + offset_vec * (dot_force * inverse3)[None],
        axis=(1, 4),
    )
    return summed * stokes_scale


def rows_to_tiles(rows, count):
    return rows.reshape(count, TILE, 3, NODES).transpose(2, 0, 1, 3).reshape(3, count, TILE * NODES)


def from_tiles(values, count):
    return (
        values.reshape(3, count, TILE, NODES).transpose(0, 3, 1, 2).reshape(3, NODES, count * TILE)
    )


def apply_blocks(blocks, flat_forces):
    return jnp.sum(blocks.astype(jnp.float32) * flat_forces[None], axis=1)


def sectioned_move(states, cut_lists):
    levels = cut_lists.shape[0]
    for section_no in range(levels):
        chosen = cut_lists[section_no]
        arrived = swapped(jnp.take(states, chosen, axis=0), "slab", levels - 1 - section_no)
        states = states.at[chosen].set(arrived)
    return states


def on_device(positions, forces, self_blocks, cut_lists, pair_tiles):
    fibres = positions.shape[2]
    unknowns = 3 * NODES
    flat_forces = forces.reshape(unknowns, fibres)
    states = jnp.concatenate(
        [positions.reshape(unknowns, fibres), flat_forces, apply_blocks(self_blocks, flat_forces)],
        axis=0,
    ).T
    states = sectioned_move(states, cut_lists)
    self_velocity = states[:, 2 * unknowns :].T
    tiles_count = fibres // TILE
    tiles = jnp.concatenate(
        [
            rows_to_tiles(states[:, :unknowns], tiles_count),
            rows_to_tiles(states[:, unknowns : 2 * unknowns], tiles_count),
        ],
        axis=0,
    )
    slab_count = lax.axis_size("slab")
    bis_count = lax.axis_size("bis")
    present = pair_tiles >= 0
    safe_ids = jnp.maximum(pair_tiles, 0)
    tile_local = safe_ids % tiles_count
    relative = (safe_ids // tiles_count // slab_count - lax.axis_index("bis")) % bis_count
    extended = with_halo(tiles, (("bis", 1),), tiles_count)
    lookup = jnp.where(
        relative == 0,
        tiles_count + tile_local,
        jnp.where(relative == 1, 2 * tiles_count + tile_local, tile_local),
    )
    lookup = jnp.clip(jnp.where(present, lookup, 0), 0, extended.shape[1] - 1)
    weights = present.astype(jnp.float32)
    targets = tiles[:3]
    tile_nodes = tiles.shape[2]
    entries = lookup.shape[0]
    all_sources = jnp.take(extended, lookup.reshape(-1), axis=1).reshape(
        6, entries, tiles_count, tile_nodes
    )
    block_len = math.gcd(tiles_count, 16)

    def stokes_block(block_no):
        first_tile = block_no * block_len
        mask_part = lax.dynamic_slice_in_dim(weights, first_tile, block_len, axis=1)
        sources = lax.dynamic_slice_in_dim(all_sources, first_tile, block_len, axis=2)
        near = lax.dynamic_slice_in_dim(targets, first_tile, block_len, axis=1)
        return stokeslet(near, sources[:3], sources[3:], mask_part)

    swept = lax.map(stokes_block, jnp.arange(tiles_count // block_len, dtype=jnp.int32))
    stokes_velocity = swept.transpose(1, 0, 2, 3).reshape(3, tiles_count, tile_nodes)
    return self_velocity.reshape(3, NODES, fibres) + from_tiles(stokes_velocity, tiles_count)


def solution(mesh):
    placed = (
        P(None, None, ("bis", "slab")),
        P(None, None, ("bis", "slab")),
        P(None, None, ("bis", "slab")),
        P(None, ("bis", "slab")),
        P(None, ("bis", "slab")),
    )
    return jax.shard_map(
        on_device,
        mesh=mesh,
        in_specs=placed,
        out_specs=P(None, None, ("bis", "slab")),
        check_vma=False,
    )
```

profile of v0, /device:TPU:1, one launch (start us, length us, event | category | flops | bytes accessed | tf_op | source)
XLA Modules:
  0.0 342.6 jit_solution(1396990577149283823)
XLA Ops:
  2.0 8.9 %multiply_reduce_fusion = f32[96,1024]{1,0:T(8,128)S(1)} fusion(bf16[96,96,1024]{2,1,0:T(8,128)(2,1)} %param.11, f32[96,1024]{1,0:T(8,128)} %bitcast.56), kind=kLoop, calls=%fused_computation.22 | loop fusion | flops 28213248 | bytes 19660800 | tf_op jit(solution)/shard_map/reduce_sum | solution.py:64
  13.1 3.2 collective-permute-start
  16.4 17.2 %collective-permute-done = f32[256,288]{1,0:T(8,128)S(1)} collective-permute-done((f32[256,288]{1,0:T(8,128)S(1)}, f32[256,288]{1,0:T(8,128)S(1)}, u32[]{:S(2)}, u32[]{:S(2)}) %collective-permute-start) | collective-permute-done | bytes 294944 | tf_op jit(solution)/shard_map/ppermute | solution.py:23
  33.6 2.0 scatter_fusion
  37.9 8.2 %collective-permute-done.1 = f32[256,288]{1,0:T(8,128)S(1)} collective-permute-done((f32[256,288]{1,0:T(8,128)S(1)}, f32[256,288]{1,0:T(8,128)S(1)}, u32[]{:S(2)}, u32[]{:S(2)}) %collective-permute-start.1) | collective-permute-done | bytes 294944 | tf_op jit(solution)/shard_map/ppermute | solution.py:23
  46.1 2.0 scatter_fusion.1
  50.3 7.4 %collective-permute-done.2 = f32[256,288]{1,0:T(8,128)S(1)} collective-permute-done((f32[256,288]{1,0:T(8,128)S(1)}, f32[256,288]{1,0:T(8,128)S(1)}, u32[]{:S(2)}, u32[]{:S(2)}) %collective-permute-start.2) | collective-permute-done | bytes 294944 | tf_op jit(solution)/shard_map/ppermute | solution.py:23
  57.8 2.0 scatter_fusion.2
  62.6 2.5 reshape.186
  68.1 3.1 collective-permute-start.4
  74.2 15.9 %collective-permute-done.4 = f32[6,256,128]{2,1,0:T(8,128)} collective-permute-done((f32[6,256,128]{2,1,0:T(8,128)S(1)}, f32[6,256,128]{2,1,0:T(8,128)}, u32[]{:S(2)}, u32[]{:S(2)}) %collective-permute-start.4) | collective-permute-done | bytes 786464 | tf_op jit(solution)/shard_map/ppermute | solution.py:35
  90.1 1.6 copy.50
  92.2 1.6 pad_maximum_fusion
  93.9 9.0 %gather_fusion = f32[1024,6,128]{2,1,0:T(8,128)} fusion(f32[6,768,128]{2,0,1:T(8,128)S(1)} %pad_maximum_fusion, s32[1024]{0:T(1024)S(1)} %broadcast_clamp_fusion), kind=kCustom, calls=%fused_computation.3 | custom fusion | bytes 6295552 | tf_op jit(solution)/shard_map/jit(_take)/gather | solution.py:111
  102.9 3.0 copy_select_fusion
  105.8 234.7 %while.10 = (s32[]{:T(128)}, f32[16,3,16,128]{3,2,1,0:T(8,128)S(1)}, s32[16]{0:T(128)S(1)}, f32[6,4,256,128]{3,2,1,0:T(8,128)S(1)}, f32[3,256,128]{2,1,0:T(8,128...) while((s32[]{:T(128)}, ...), condition=%wide.region_8.10_spmd, body=%wide.region_4.9_spmd.sunk | while | flops 34603016 | bytes 34513868 | solution.py:123
  108.0 6.8 %fusion.20 = (f32[4,16,128,128]{3,2,1,0:T(8,128)S(1)}, f32[4,16,128,128]{3,2,1,0:T(8,128)S(1)}) fusion(f32[3,4,16,128]{3,2,1,0:T(8,128)S(1)} %get-tuple-element.130, f32[3,16,128]{2,1,0:T(8,128)S(1)} %constant_dynamic-slice_fusion.8, f32[3,4,16,128]{3,2,1,0:T(8,128)S(1)} %get-tuple-element.131), kind=kLoop, calls=%fused_computation.10.clone.1 | loop fusion | flops 13631488 | bytes 8609792 | tf_op jit(solution)/shard_map/while/body/eval_jaxpr/reduce_sum | solution.py:42
  114.8 1.9 fusion.21
  116.7 3.8 %fusion.22 = f32[3,16,128]{2,1,0:T(8,128)S(1)} fusion(f32[4,16,128,128]{3,2,1,0:T(8,128)S(1)} %get-tuple-element.134, f32[4,16,128,128]{3,2,1,0:T(8,128)S(1)} %get-tuple-element.135, f32[3,4,16,128]{3,2,1,0:T(8,128)S(1)} %get-tuple-element.130, f32[3,16,128]{2,1,0:T(8,128)S(1)} %constant_dynamic-slice_fusion.8, ...), kind=kLoop, calls=%fused_computation.13.clone.1 | loop fusion | flops 15722496 | bytes 8634368 | tf_op jit(solution)/shard_map/while/body/eval_jaxpr/reduce_sum | solution.py:46
  122.6 6.8 %fusion.20 = (f32[4,16,128,128]{3,2,1,0:T(8,128)S(1)}, f32[4,16,128,128]{3,2,1,0:T(8,128)S(1)}) fusion(f32[3,4,16,128]{3,2,1,0:T(8,128)S(1)} %get-tuple-element.130, f32[3,16,128]{2,1,0:T(8,128)S(1)} %constant_dynamic-slice_fusion.8, f32[3,4,16,128]{3,2,1,0:T(8,128)S(1)} %get-tuple-element.131), kind=kLoop, calls=%fused_computation.10.clone.1 | loop fusion | flops 13631488 | bytes 8609792 | tf_op jit(solution)/shard_map/while/body/eval_jaxpr/reduce_sum | solution.py:42
  129.4 1.9 fusion.21
  131.3 3.8 %fusion.22 = f32[3,16,128]{2,1,0:T(8,128)S(1)} fusion(f32[4,16,128,128]{3,2,1,0:T(8,128)S(1)} %get-tuple-element.134, f32[4,16,128,128]{3,2,1,0:T(8,128)S(1)} %get-tuple-element.135, f32[3,4,16,128]{3,2,1,0:T(8,128)S(1)} %get-tuple-element.130, f32[3,16,128]{2,1,0:T(8,128)S(1)} %constant_dynamic-slice_fusion.8, ...), kind=kLoop, calls=%fused_computation.13.clone.1 | loop fusion | flops 15722496 | bytes 8634368 | tf_op jit(solution)/shard_map/while/body/eval_jaxpr/reduce_sum | solution.py:46
  137.3 6.8 %fusion.20 = (f32[4,16,128,128]{3,2,1,0:T(8,128)S(1)}, f32[4,16,128,128]{3,2,1,0:T(8,128)S(1)}) fusion(f32[3,4,16,128]{3,2,1,0:T(8,128)S(1)} %get-tuple-element.130, f32[3,16,128]{2,1,0:T(8,128)S(1)} %constant_dynamic-slice_fusion.8, f32[3,4,16,128]{3,2,1,0:T(8,128)S(1)} %get-tuple-element.131), kind=kLoop, calls=%fused_computation.10.clone.1 | loop fusion | flops 13631488 | bytes 8609792 | tf_op jit(solution)/shard_map/while/body/eval_jaxpr/reduce_sum | solution.py:42
  144.1 1.9 fusion.21
  146.0 3.8 %fusion.22 = f32[3,16,128]{2,1,0:T(8,128)S(1)} fusion(f32[4,16,128,128]{3,2,1,0:T(8,128)S(1)} %get-tuple-element.134, f32[4,16,128,128]{3,2,1,0:T(8,128)S(1)} %get-tuple-element.135, f32[3,4,16,128]{3,2,1,0:T(8,128)S(1)} %get-tuple-element.130, f32[3,16,128]{2,1,0:T(8,128)S(1)} %constant_dynamic-slice_fusion.8, ...), kind=kLoop, calls=%fused_computation.13.clone.1 | loop fusion | flops 15722496 | bytes 8634368 | tf_op jit(solution)/shard_map/while/body/eval_jaxpr/reduce_sum | solution.py:46
  152.0 6.8 %fusion.20 = (f32[4,16,128,128]{3,2,1,0:T(8,128)S(1)}, f32[4,16,128,128]{3,2,1,0:T(8,128)S(1)}) fusion(f32[3,4,16,128]{3,2,1,0:T(8,128)S(1)} %get-tuple-element.130, f32[3,16,128]{2,1,0:T(8,128)S(1)} %constant_dynamic-slice_fusion.8, f32[3,4,16,128]{3,2,1,0:T(8,128)S(1)} %get-tuple-element.131), kind=kLoop, calls=%fused_computation.10.clone.1 | loop fusion | flops 13631488 | bytes 8609792 | tf_op jit(solution)/shard_map/while/body/eval_jaxpr/reduce_sum | solution.py:42
  158.8 1.9 fusion.21
  160.7 3.8 %fusion.22 = f32[3,16,128]{2,1,0:T(8,128)S(1)} fusion(f32[4,16,128,128]{3,2,1,0:T(8,128)S(1)} %get-tuple-element.134, f32[4,16,128,128]{3,2,1,0:T(8,128)S(1)} %get-tuple-element.135, f32[3,4,16,128]{3,2,1,0:T(8,128)S(1)} %get-tuple-element.130, f32[3,16,128]{2,1,0:T(8,128)S(1)} %constant_dynamic-slice_fusion.8, ...), kind=kLoop, calls=%fused_computation.13.clone.1 | loop fusion | flops 15722496 | bytes 8634368 | tf_op jit(solution)/shard_map/while/body/eval_jaxpr/reduce_sum | solution.py:46
  166.7 6.8 %fusion.20 = (f32[4,16,128,128]{3,2,1,0:T(8,128)S(1)}, f32[4,16,128,128]{3,2,1,0:T(8,128)S(1)}) fusion(f32[3,4,16,128]{3,2,1,0:T(8,128)S(1)} %get-tuple-element.130, f32[3,16,128]{2,1,0:T(8,128)S(1)} %constant_dynamic-slice_fusion.8, f32[3,4,16,128]{3,2,1,0:T(8,128)S(1)} %get-tuple-element.131), kind=kLoop, calls=%fused_computation.10.clone.1 | loop fusion | flops 13631488 | bytes 8609792 | tf_op jit(solution)/shard_map/while/body/eval_jaxpr/reduce_sum | solution.py:42
  173.5 1.9 fusion.21
  175.3 3.8 %fusion.22 = f32[3,16,128]{2,1,0:T(8,128)S(1)} fusion(f32[4,16,128,128]{3,2,1,0:T(8,128)S(1)} %get-tuple-element.134, f32[4,16,128,128]{3,2,1,0:T(8,128)S(1)} %get-tuple-element.135, f32[3,4,16,128]{3,2,1,0:T(8,128)S(1)} %get-tuple-element.130, f32[3,16,128]{2,1,0:T(8,128)S(1)} %constant_dynamic-slice_fusion.8, ...), kind=kLoop, calls=%fused_computation.13.clone.1 | loop fusion | flops 15722496 | bytes 8634368 | tf_op jit(solution)/shard_map/while/body/eval_jaxpr/reduce_sum | solution.py:46
  181.3 6.8 %fusion.20 = (f32[4,16,128,128]{3,2,1,0:T(8,128)S(1)}, f32[4,16,128,128]{3,2,1,0:T(8,128)S(1)}) fusion(f32[3,4,16,128]{3,2,1,0:T(8,128)S(1)} %get-tuple-element.130, f32[3,16,128]{2,1,0:T(8,128)S(1)} %constant_dynamic-slice_fusion.8, f32[3,4,16,128]{3,2,1,0:T(8,128)S(1)} %get-tuple-element.131), kind=kLoop, calls=%fused_computation.10.clone.1 | loop fusion | flops 13631488 | bytes 8609792 | tf_op jit(solution)/shard_map/while/body/eval_jaxpr/reduce_sum | solution.py:42
  188.1 1.9 fusion.21
  190.0 3.8 %fusion.22 = f32[3,16,128]{2,1,0:T(8,128)S(1)} fusion(f32[4,16,128,128]{3,2,1,0:T(8,128)S(1)} %get-tuple-element.134, f32[4,16,128,128]{3,2,1,0:T(8,128)S(1)} %get-tuple-element.135, f32[3,4,16,128]{3,2,1,0:T(8,128)S(1)} %get-tuple-element.130, f32[3,16,128]{2,1,0:T(8,128)S(1)} %constant_dynamic-slice_fusion.8, ...), kind=kLoop, calls=%fused_computation.13.clone.1 | loop fusion | flops 15722496 | bytes 8634368 | tf_op jit(solution)/shard_map/while/body/eval_jaxpr/reduce_sum | solution.py:46
  196.0 6.8 %fusion.20 = (f32[4,16,128,128]{3,2,1,0:T(8,128)S(1)}, f32[4,16,128,128]{3,2,1,0:T(8,128)S(1)}) fusion(f32[3,4,16,128]{3,2,1,0:T(8,128)S(1)} %get-tuple-element.130, f32[3,16,128]{2,1,0:T(8,128)S(1)} %constant_dynamic-slice_fusion.8, f32[3,4,16,128]{3,2,1,0:T(8,128)S(1)} %get-tuple-element.131), kind=kLoop, calls=%fused_computation.10.clone.1 | loop fusion | flops 13631488 | bytes 8609792 | tf_op jit(solution)/shard_map/while/body/eval_jaxpr/reduce_sum | solution.py:42
  202.8 1.9 fusion.21
  204.7 3.8 %fusion.22 = f32[3,16,128]{2,1,0:T(8,128)S(1)} fusion(f32[4,16,128,128]{3,2,1,0:T(8,128)S(1)} %get-tuple-element.134, f32[4,16,128,128]{3,2,1,0:T(8,128)S(1)} %get-tuple-element.135, f32[3,4,16,128]{3,2,1,0:T(8,128)S(1)} %get-tuple-element.130, f32[3,16,128]{2,1,0:T(8,128)S(1)} %constant_dynamic-slice_fusion.8, ...), kind=kLoop, calls=%fused_computation.13.clone.1 | loop fusion | flops 15722496 | bytes 8634368 | tf_op jit(solution)/shard_map/while/body/eval_jaxpr/reduce_sum | solution.py:46
  210.7 6.8 %fusion.20 = (f32[4,16,128,128]{3,2,1,0:T(8,128)S(1)}, f32[4,16,128,128]{3,2,1,0:T(8,128)S(1)}) fusion(f32[3,4,16,128]{3,2,1,0:T(8,128)S(1)} %get-tuple-element.130, f32[3,16,128]{2,1,0:T(8,128)S(1)} %constant_dynamic-slice_fusion.8, f32[3,4,16,128]{3,2,1,0:T(8,128)S(1)} %get-tuple-element.131), kind=kLoop, calls=%fused_computation.10.clone.1 | loop fusion | flops 13631488 | bytes 8609792 | tf_op jit(solution)/shard_map/while/body/eval_jaxpr/reduce_sum | solution.py:42
  217.5 1.9 fusion.21
  219.3 3.8 %fusion.22 = f32[3,16,128]{2,1,0:T(8,128)S(1)} fusion(f32[4,16,128,128]{3,2,1,0:T(8,128)S(1)} %get-tuple-element.134, f32[4,16,128,128]{3,2,1,0:T(8,128)S(1)} %get-tuple-element.135, f32[3,4,16,128]{3,2,1,0:T(8,128)S(1)} %get-tuple-element.130, f32[3,16,128]{2,1,0:T(8,128)S(1)} %constant_dynamic-slice_fusion.8, ...), kind=kLoop, calls=%fused_computation.13.clone.1 | loop fusion | flops 15722496 | bytes 8634368 | tf_op jit(solution)/shard_map/while/body/eval_jaxpr/reduce_sum | solution.py:46
  225.3 6.8 %fusion.20 = (f32[4,16,128,128]{3,2,1,0:T(8,128)S(1)}, f32[4,16,128,128]{3,2,1,0:T(8,128)S(1)}) fusion(f32[3,4,16,128]{3,2,1,0:T(8,128)S(1)} %get-tuple-element.130, f32[3,16,128]{2,1,0:T(8,128)S(1)} %constant_dynamic-slice_fusion.8, f32[3,4,16,128]{3,2,1,0:T(8,128)S(1)} %get-tuple-element.131), kind=kLoop, calls=%fused_computation.10.clone.1 | loop fusion | flops 13631488 | bytes 8609792 | tf_op jit(solution)/shard_map/while/body/eval_jaxpr/reduce_sum | solution.py:42
  232.1 1.9 fusion.21
  234.0 3.8 %fusion.22 = f32[3,16,128]{2,1,0:T(8,128)S(1)} fusion(f32[4,16,128,128]{3,2,1,0:T(8,128)S(1)} %get-tuple-element.134, f32[4,16,128,128]{3,2,1,0:T(8,128)S(1)} %get-tuple-element.135, f32[3,4,16,128]{3,2,1,0:T(8,128)S(1)} %get-tuple-element.130, f32[3,16,128]{2,1,0:T(8,128)S(1)} %constant_dynamic-slice_fusion.8, ...), kind=kLoop, calls=%fused_computation.13.clone.1 | loop fusion | flops 15722496 | bytes 8634368 | tf_op jit(solution)/shard_map/while/body/eval_jaxpr/reduce_sum | solution.py:46
  240.0 6.8 %fusion.20 = (f32[4,16,128,128]{3,2,1,0:T(8,128)S(1)}, f32[4,16,128,128]{3,2,1,0:T(8,128)S(1)}) fusion(f32[3,4,16,128]{3,2,1,0:T(8,128)S(1)} %get-tuple-element.130, f32[3,16,128]{2,1,0:T(8,128)S(1)} %constant_dynamic-slice_fusion.8, f32[3,4,16,128]{3,2,1,0:T(8,128)S(1)} %get-tuple-element.131), kind=kLoop, calls=%fused_computation.10.clone.1 | loop fusion | flops 13631488 | bytes 8609792 | tf_op jit(solution)/shard_map/while/body/eval_jaxpr/reduce_sum | solution.py:42
  246.8 1.9 fusion.21
  248.7 3.8 %fusion.22 = f32[3,16,128]{2,1,0:T(8,128)S(1)} fusion(f32[4,16,128,128]{3,2,1,0:T(8,128)S(1)} %get-tuple-element.134, f32[4,16,128,128]{3,2,1,0:T(8,128)S(1)} %get-tuple-element.135, f32[3,4,16,128]{3,2,1,0:T(8,128)S(1)} %get-tuple-element.130, f32[3,16,128]{2,1,0:T(8,128)S(1)} %constant_dynamic-slice_fusion.8, ...), kind=kLoop, calls=%fused_computation.13.clone.1 | loop fusion | flops 15722496 | bytes 8634368 | tf_op jit(solution)/shard_map/while/body/eval_jaxpr/reduce_sum | solution.py:46
  254.7 6.8 %fusion.20 = (f32[4,16,128,128]{3,2,1,0:T(8,128)S(1)}, f32[4,16,128,128]{3,2,1,0:T(8,128)S(1)}) fusion(f32[3,4,16,128]{3,2,1,0:T(8,128)S(1)} %get-tuple-element.130, f32[3,16,128]{2,1,0:T(8,128)S(1)} %constant_dynamic-slice_fusion.8, f32[3,4,16,128]{3,2,1,0:T(8,128)S(1)} %get-tuple-element.131), kind=kLoop, calls=%fused_computation.10.clone.1 | loop fusion | flops 13631488 | bytes 8609792 | tf_op jit(solution)/shard_map/while/body/eval_jaxpr/reduce_sum | solution.py:42
  261.5 1.9 fusion.21
  263.4 3.8 %fusion.22 = f32[3,16,128]{2,1,0:T(8,128)S(1)} fusion(f32[4,16,128,128]{3,2,1,0:T(8,128)S(1)} %get-tuple-element.134, f32[4,16,128,128]{3,2,1,0:T(8,128)S(1)} %get-tuple-element.135, f32[3,4,16,128]{3,2,1,0:T(8,128)S(1)} %get-tuple-element.130, f32[3,16,128]{2,1,0:T(8,128)S(1)} %constant_dynamic-slice_fusion.8, ...), kind=kLoop, calls=%fused_computation.13.clone.1 | loop fusion | flops 15722496 | bytes 8634368 | tf_op jit(solution)/shard_map/while/body/eval_jaxpr/reduce_sum | solution.py:46
  269.3 6.8 %fusion.20 = (f32[4,16,128,128]{3,2,1,0:T(8,128)S(1)}, f32[4,16,128,128]{3,2,1,0:T(8,128)S(1)}) fusion(f32[3,4,16,128]{3,2,1,0:T(8,128)S(1)} %get-tuple-element.130, f32[3,16,128]{2,1,0:T(8,128)S(1)} %constant_dynamic-slice_fusion.8, f32[3,4,16,128]{3,2,1,0:T(8,128)S(1)} %get-tuple-element.131), kind=kLoop, calls=%fused_computation.10.clone.1 | loop fusion | flops 13631488 | bytes 8609792 | tf_op jit(solution)/shard_map/while/body/eval_jaxpr/reduce_sum | solution.py:42
  276.2 1.9 fusion.21
  278.0 3.8 %fusion.22 = f32[3,16,128]{2,1,0:T(8,128)S(1)} fusion(f32[4,16,128,128]{3,2,1,0:T(8,128)S(1)} %get-tuple-element.134, f32[4,16,128,128]{3,2,1,0:T(8,128)S(1)} %get-tuple-element.135, f32[3,4,16,128]{3,2,1,0:T(8,128)S(1)} %get-tuple-element.130, f32[3,16,128]{2,1,0:T(8,128)S(1)} %constant_dynamic-slice_fusion.8, ...), kind=kLoop, calls=%fused_computation.13.clone.1 | loop fusion | flops 15722496 | bytes 8634368 | tf_op jit(solution)/shard_map/while/body/eval_jaxpr/reduce_sum | solution.py:46
  284.0 6.8 %fusion.20 = (f32[4,16,128,128]{3,2,1,0:T(8,128)S(1)}, f32[4,16,128,128]{3,2,1,0:T(8,128)S(1)}) fusion(f32[3,4,16,128]{3,2,1,0:T(8,128)S(1)} %get-tuple-element.130, f32[3,16,128]{2,1,0:T(8,128)S(1)} %constant_dynamic-slice_fusion.8, f32[3,4,16,128]{3,2,1,0:T(8,128)S(1)} %get-tuple-element.131), kind=kLoop, calls=%fused_computation.10.clone.1 | loop fusion | flops 13631488 | bytes 8609792 | tf_op jit(solution)/shard_map/while/body/eval_jaxpr/reduce_sum | solution.py:42
  290.8 1.9 fusion.21
  292.7 3.8 %fusion.22 = f32[3,16,128]{2,1,0:T(8,128)S(1)} fusion(f32[4,16,128,128]{3,2,1,0:T(8,128)S(1)} %get-tuple-element.134, f32[4,16,128,128]{3,2,1,0:T(8,128)S(1)} %get-tuple-element.135, f32[3,4,16,128]{3,2,1,0:T(8,128)S(1)} %get-tuple-element.130, f32[3,16,128]{2,1,0:T(8,128)S(1)} %constant_dynamic-slice_fusion.8, ...), kind=kLoop, calls=%fused_computation.13.clone.1 | loop fusion | flops 15722496 | bytes 8634368 | tf_op jit(solution)/shard_map/while/body/eval_jaxpr/reduce_sum | solution.py:46
  298.7 6.8 %fusion.20 = (f32[4,16,128,128]{3,2,1,0:T(8,128)S(1)}, f32[4,16,128,128]{3,2,1,0:T(8,128)S(1)}) fusion(f32[3,4,16,128]{3,2,1,0:T(8,128)S(1)} %get-tuple-element.130, f32[3,16,128]{2,1,0:T(8,128)S(1)} %constant_dynamic-slice_fusion.8, f32[3,4,16,128]{3,2,1,0:T(8,128)S(1)} %get-tuple-element.131), kind=kLoop, calls=%fused_computation.10.clone.1 | loop fusion | flops 13631488 | bytes 8609792 | tf_op jit(solution)/shard_map/while/body/eval_jaxpr/reduce_sum | solution.py:42
  305.5 1.9 fusion.21
  307.4 3.8 %fusion.22 = f32[3,16,128]{2,1,0:T(8,128)S(1)} fusion(f32[4,16,128,128]{3,2,1,0:T(8,128)S(1)} %get-tuple-element.134, f32[4,16,128,128]{3,2,1,0:T(8,128)S(1)} %get-tuple-element.135, f32[3,4,16,128]{3,2,1,0:T(8,128)S(1)} %get-tuple-element.130, f32[3,16,128]{2,1,0:T(8,128)S(1)} %constant_dynamic-slice_fusion.8, ...), kind=kLoop, calls=%fused_computation.13.clone.1 | loop fusion | flops 15722496 | bytes 8634368 | tf_op jit(solution)/shard_map/while/body/eval_jaxpr/reduce_sum | solution.py:46
  313.4 6.8 %fusion.20 = (f32[4,16,128,128]{3,2,1,0:T(8,128)S(1)}, f32[4,16,128,128]{3,2,1,0:T(8,128)S(1)}) fusion(f32[3,4,16,128]{3,2,1,0:T(8,128)S(1)} %get-tuple-element.130, f32[3,16,128]{2,1,0:T(8,128)S(1)} %constant_dynamic-slice_fusion.8, f32[3,4,16,128]{3,2,1,0:T(8,128)S(1)} %get-tuple-element.131), kind=kLoop, calls=%fused_computation.10.clone.1 | loop fusion | flops 13631488 | bytes 8609792 | tf_op jit(solution)/shard_map/while/body/eval_jaxpr/reduce_sum | solution.py:42
  320.2 1.9 fusion.21
  322.0 3.8 %fusion.22 = f32[3,16,128]{2,1,0:T(8,128)S(1)} fusion(f32[4,16,128,128]{3,2,1,0:T(8,128)S(1)} %get-tuple-element.134, f32[4,16,128,128]{3,2,1,0:T(8,128)S(1)} %get-tuple-element.135, f32[3,4,16,128]{3,2,1,0:T(8,128)S(1)} %get-tuple-element.130, f32[3,16,128]{2,1,0:T(8,128)S(1)} %constant_dynamic-slice_fusion.8, ...), kind=kLoop, calls=%fused_computation.13.clone.1 | loop fusion | flops 15722496 | bytes 8634368 | tf_op jit(solution)/shard_map/while/body/eval_jaxpr/reduce_sum | solution.py:46
  328.0 6.8 %fusion.20 = (f32[4,16,128,128]{3,2,1,0:T(8,128)S(1)}, f32[4,16,128,128]{3,2,1,0:T(8,128)S(1)}) fusion(f32[3,4,16,128]{3,2,1,0:T(8,128)S(1)} %get-tuple-element.130, f32[3,16,128]{2,1,0:T(8,128)S(1)} %constant_dynamic-slice_fusion.8, f32[3,4,16,128]{3,2,1,0:T(8,128)S(1)} %get-tuple-element.131), kind=kLoop, calls=%fused_computation.10.clone.1 | loop fusion | flops 13631488 | bytes 8609792 | tf_op jit(solution)/shard_map/while/body/eval_jaxpr/reduce_sum | solution.py:42
  334.8 1.9 fusion.21
  336.7 3.8 %fusion.22 = f32[3,16,128]{2,1,0:T(8,128)S(1)} fusion(f32[4,16,128,128]{3,2,1,0:T(8,128)S(1)} %get-tuple-element.134, f32[4,16,128,128]{3,2,1,0:T(8,128)S(1)} %get-tuple-element.135, f32[3,4,16,128]{3,2,1,0:T(8,128)S(1)} %get-tuple-element.130, f32[3,16,128]{2,1,0:T(8,128)S(1)} %constant_dynamic-slice_fusion.8, ...), kind=kLoop, calls=%fused_computation.13.clone.1 | loop fusion | flops 15722496 | bytes 8634368 | tf_op jit(solution)/shard_map/while/body/eval_jaxpr/reduce_sum | solution.py:46
  (140 shorter events, 43.5 us)
Async XLA Ops:
  2.0 9.1 %copy-start.3 = (f32[3,32,1024]{2,1,0:T(8,128)S(1)}, f32[3,32,1024]{2,1,0:T(8,128)}, u32[]{:S(2)}) copy-start(f32[3,32,1024]{2,1,0:T(8,128)} %param.9) | copy-start | bytes 1179652
  11.2 5.2 %copy-start.5 = (s32[3,256]{1,0:T(4,128)S(1)}, s32[3,256]{1,0:T(4,128)}, u32[]{:S(2)}) copy-start(s32[3,256]{1,0:T(4,128)} %param.12) | copy-start | bytes 9220
  13.1 20.5 %collective-permute-start = (f32[256,288]{1,0:T(8,128)S(1)}, f32[256,288]{1,0:T(8,128)S(1)}, u32[]{:S(2)}, u32[]{:S(2)}) collective-permute-start(f32[256,288]{1,0:T(8,128)S(1)} %broadcast_select_fusion.2), channel_id=1, source_target_pairs={{0,4},{4,0},{1,5},{5,1},{2,6},{6,2},{3,7},{7,3},{8,12},{12,8},{9,1... | collective-permute-start | bytes 884744 | tf_op jit(solution)/shard_map/ppermute | solution.py:23
  36.7 9.4 %collective-permute-start.1 = (f32[256,288]{1,0:T(8,128)S(1)}, f32[256,288]{1,0:T(8,128)S(1)}, u32[]{:S(2)}, u32[]{:S(2)}) collective-permute-start(f32[256,288]{1,0:T(8,128)S(1)} %broadcast_select_fusion.1), channel_id=1, source_target_pairs={{0,2},{2,0},{1,3},{3,1},{4,6},{6,4},{5,7},{7,5},{8,10},{10,8},{9,1... | collective-permute-start | bytes 884744 | tf_op jit(solution)/shard_map/ppermute | solution.py:23
  49.2 8.5 %collective-permute-start.2 = (f32[256,288]{1,0:T(8,128)S(1)}, f32[256,288]{1,0:T(8,128)S(1)}, u32[]{:S(2)}, u32[]{:S(2)}) collective-permute-start(f32[256,288]{1,0:T(8,128)S(1)} %broadcast_select_fusion), channel_id=1, source_target_pairs={{0,1},{1,0},{2,3},{3,2},{4,5},{5,4},{6,7},{7,6},{8,9},{9,8},{10,11... | collective-permute-start | bytes 884744 | tf_op jit(solution)/shard_map/ppermute | solution.py:23
  62.6 5.5 %copy-start = (f32[3,256,128]{2,0,1:T(4,128)}, f32[3,256,128]{2,0,1:T(4,128)S(1)}, u32[]{:S(2)}) copy-start(f32[3,256,128]{2,0,1:T(4,128)S(1)} %copy.45) | copy-start | bytes 1179652
  65.1 7.2 %copy-start.6 = (s32[4,256]{1,0:T(4,128)S(1)}, s32[4,256]{1,0:T(4,128)}, u32[]{:S(2)}) copy-start(s32[4,256]{1,0:T(4,128)} %param.13) | copy-start | bytes 12292
  67.7 24.1 %copy-start.1 = (f32[3,256,128]{2,0,1:T(4,128)}, f32[3,256,128]{2,0,1:T(4,128)S(1)}, u32[]{:S(2)}) copy-start(f32[3,256,128]{2,0,1:T(4,128)S(1)} %copy.46) | copy-start | bytes 1179652
  68.1 22.1 %collective-permute-start.4 = (f32[6,256,128]{2,1,0:T(8,128)S(1)}, f32[6,256,128]{2,1,0:T(8,128)}, u32[]{:S(2)}, u32[]{:S(2)}) collective-permute-start(f32[6,256,128]{2,1,0:T(8,128)S(1)} %copy.47), channel_id=1, source_target_pairs={{8,0},{16,8},{24,16},{0,24},{9,1},{17,9},{25,17},{1,25},{10,2},{18... | collective-permute-start | bytes 2359304 | tf_op jit(solution)/shard_map/ppermute | solution.py:35
  71.2 20.6 %collective-permute-start.3 = (f32[6,256,128]{2,1,0:T(8,128)S(1)}, f32[6,256,128]{2,1,0:T(8,128)S(1)}, u32[]{:S(2)}, u32[]{:S(2)}) collective-permute-start(f32[6,256,128]{2,1,0:T(8,128)S(1)} %copy.47), channel_id=1, source_target_pairs={{0,8},{8,16},{16,24},{24,0},{1,9},{9,17},{17,25},{25,1},{2,10},{10... | collective-permute-start | bytes 2359304 | tf_op jit(solution)/shard_map/ppermute | solution.py:32
  102.9 3.0 copy-start.4
  340.6 1.2 copy-start.2
where the time goes:
time: 345 us; the launch traced here: 343 us
  other arithmetic  216 us (63%)
  local copies, waits for them, and re-layouts  57 us (17%)
  waiting for transfers between devices  48.7 us (14%)
  loops' own time  11 us (3%)
  starting transfers between devices  9.79 us (3%)
    reduce_sum x16, other arithmetic, stokeslet(): radius2 = jnp.sum(offset_vec * offset_vec, axis=0) + blob_eps2  109 us
    reduce_sum x16, other arithmetic, stokeslet(): jnp.sum(pushes[:, :, :, None, :] * inverse[None] + offset_vec * (dot_forc...  61.4 us
    ppermute x3, waiting for transfers between devices, swapped(): return lax.ppermute(block, axis, route)  32.8 us
    mul x16, other arithmetic, stokeslet(): dot_force * inverse3  29.8 us
    ppermute x1, waiting for transfers between devices, with_halo(): lax.ppermute(lax.slice_in_dim(block, 0, width, axis=dim), axis, backward)  15.9 us
    dynamic_slice x16, local copies, waits for them, and re-layouts, stokes_block(): near = lax.dynamic_slice_in_dim(targets, first_tile, block_len, axis=1)  11.8 us
    another operation x1, loops' own time, on_device(): lax.map(stokes_block, jnp.arange(tiles_count // block_len, dtype=jnp.int32))  11 us
    dynamic_slice x16, local copies, waits for them, and re-layouts, on_device(): lax.map(stokes_block, jnp.arange(tiles_count // block_len, dtype=jnp.int32))  10.2 us
  transfers between devices with their start and end apart: 5, of which 4 were waited for; matrix products, arithmetic and copies ran while one was open for 1% of the time, Pallas kernels for 0%

commit v1 on v0

v1 whole, which is shorter than its diff:
```python
import math, functools
import jax, jax.numpy as jnp
from jax import lax
from jax.experimental import pallas as pl
from jax.experimental.pallas import tpu as pltpu
from jax.sharding import PartitionSpec as P

NODES = 32
TILE = 4


blob_eps2 = 0.0025
stokes_scale = 1.0 / (8.0 * math.pi)


def pieces(t):
    h1 = t.astype(jnp.bfloat16).astype(jnp.float32)
    r = t - h1
    h2 = r.astype(jnp.bfloat16).astype(jnp.float32)
    h3 = (r - h2).astype(jnp.bfloat16).astype(jnp.float32)
    return h1, h2, h3


def target_features(t):
    h1, h2, h3 = pieces(t)
    row = lax.broadcasted_iota(jnp.int32, (8, 128), 0)
    zero = jnp.zeros((8, 128), jnp.float32)

    def near(h, unit):
        return jnp.where(row < 3, -2.0 * h, jnp.where(row == 6, unit, 0.0))

    def push(h, unit):
        return jnp.where(
            (row >= 3) & (row < 6), pltpu.roll(h, 3, axis=0), jnp.where(row == 7, unit, 0.0)
        )

    norm = jnp.broadcast_to(t[6:7] + blob_eps2, (8, 128))
    e1, e2, e3 = pieces(norm)
    own = jnp.where(row == 0, e1, jnp.where(row == 1, e2, jnp.where(row == 2, e3, 0.0)))
    order = [(h1, 1.0), (h1, 1.0), (h2, 0.0), (h2, 0.0), (h1, 1.0), (h3, 0.0)]
    left = jnp.concatenate([near(h, u) for h, u in order] + [own, zero], axis=0)
    right = jnp.concatenate([push(h, u) for h, u in order] + [zero, zero], axis=0)
    return jnp.concatenate([left, right], axis=1).astype(jnp.bfloat16)


def stokes_kernel(entries, look, ext, out, packed, qp0, qp1, acc0, acc1):
    count = out.shape[1]
    total = ext.shape[0]

    @pl.loop(0, total // 8)
    def _(i):
        first = pl.multiple_of(i * 8, 8)
        h1, h2, h3 = pieces(ext[pl.ds(first, 8)])
        packed[pl.ds(first, 8)] = jnp.concatenate([h1, h2, h3, h1], axis=1).astype(jnp.bfloat16)

    ones16 = jnp.ones((16, 128), jnp.bfloat16)

    def products(g, qp):
        feats = target_features(ext[g])
        for n in range(0, entries, 2):
            side = []
            for k in (n, n + 1):
                e = look[k, g]
                low = packed[e, 0:16]
                side.append(jnp.concatenate([low, low, packed[e, 16:32], ones16], axis=0))
            sources = jnp.concatenate(side, axis=1)
            qp[:, n * 128 : (n + 2) * 128] = lax.dot_general(
                feats, sources, (((0,), (0,)), ((), ())), preferred_element_type=jnp.float32
            )

    def sweep(g, qp, acc):
        ys, fs = [], []
        for n in range(entries):
            e = look[n, g]
            ys.append([jnp.broadcast_to(ext[e, i : i + 1], (8, 128)) for i in range(3)])
            fs.append([jnp.broadcast_to(ext[e, i + 3 : i + 4], (8, 128)) for i in range(3)])
        for c in range(16):
            tot = None
            for n in range(entries):
                q = qp[c * 8 : c * 8 + 8, n * 128 : n * 128 + 128]
                p = qp[128 + c * 8 : 136 + c * 8, n * 128 : n * 128 + 128]
                w = lax.rsqrt(q)
                s = p * (w * w) * w
                part = [w * fs[n][i] - s * ys[n][i] for i in range(3)] + [s]
                tot = part if tot is None else [a + b for a, b in zip(tot, part)]
            for i in range(4):
                high = tot[i].astype(jnp.bfloat16).astype(jnp.float32)
                acc[i * 128 + c * 8 : i * 128 + c * 8 + 8, 0:128] = tot[i]

    def finish(g, acc):
        a = acc[...]
        high = a.astype(jnp.bfloat16)
        low = (a - high.astype(jnp.float32)).astype(jnp.bfloat16)
        sums = lax.dot_general(
            jnp.ones((8, 256), jnp.bfloat16), jnp.concatenate([high, low], axis=1),
            (((1,), (1,)), ((), ())), preferred_element_type=jnp.float32,
        )
        t = ext[g]
        for i in range(3):
            out[i, pl.ds(g, 1)] = stokes_scale * (
                sums[0:1, i * 128 : i * 128 + 128] + t[i : i + 1] * sums[0:1, 384:512]
            )

    products(0, qp0)

    @pl.loop(0, count // 2)
    def _(h):
        g = h * 2
        products(g + 1, qp1)
        sweep(g, qp0, acc0)
        products(jnp.minimum(g + 2, count - 1), qp0)
        finish(g, acc0)
        sweep(g + 1, qp1, acc1)
        finish(g + 1, acc1)


def stokes_tiles(ext, look):
    entries, count = look.shape
    total = ext.shape[0]
    return pl.pallas_call(
        functools.partial(stokes_kernel, entries),
        out_shape=jax.ShapeDtypeStruct((3, count, 128), jnp.float32),
        in_specs=[pl.BlockSpec(memory_space=pltpu.SMEM), pl.BlockSpec(memory_space=pltpu.VMEM)],
        out_specs=pl.BlockSpec(memory_space=pltpu.VMEM),
        scratch_shapes=[
            pltpu.VMEM((total, 32, 128), jnp.bfloat16),
            pltpu.VMEM((256, entries * 128), jnp.float32),
            pltpu.VMEM((256, entries * 128), jnp.float32),
            pltpu.VMEM((512, 128), jnp.float32),
            pltpu.VMEM((512, 128), jnp.float32),
        ],
        compiler_params=pltpu.CompilerParams(vmem_limit_bytes=48 * 2**20),
        cost_estimate=pl.CostEstimate(flops=400_000_000, bytes_accessed=2_000_000, transcendentals=0),
    )(look, ext)


def swapped(block, axis, distance):
    count = lax.axis_size(axis)
    route = []
    for low in range(count):
        high = low | 1 << distance
        if high != low and high < count:
            route += [(low, high), (high, low)]
    return lax.ppermute(block, axis, route)


def with_halo(block, sides, width):
    for axis, dim in sides:
        count = lax.axis_size(axis)
        forward = [(i, i + 1) for i in range(count - 1)]
        forward.append((count - 1, 0))
        backward = [(target, source) for source, target in forward]
        low = lax.ppermute(
            lax.slice_in_dim(block, block.shape[dim] - width, None, axis=dim), axis, forward
        )
        high = lax.ppermute(lax.slice_in_dim(block, 0, width, axis=dim), axis, backward)
        block = jnp.concatenate([low, block, high], axis=dim)
    return block


def rows_to_tiles(rows, count):
    return rows.reshape(count, TILE, 3, NODES).transpose(2, 0, 1, 3).reshape(3, count, TILE * NODES)


def from_tiles(values, count):
    return (
        values.reshape(3, count, TILE, NODES).transpose(0, 3, 1, 2).reshape(3, NODES, count * TILE)
    )


def apply_blocks(blocks, flat_forces):
    return jnp.sum(blocks.astype(jnp.float32) * flat_forces[None], axis=1)


def sectioned_move(states, cut_lists):
    levels = cut_lists.shape[0]
    for section_no in range(levels):
        chosen = cut_lists[section_no]
        arrived = swapped(jnp.take(states, chosen, axis=0), "slab", levels - 1 - section_no)
        states = states.at[chosen].set(arrived)
    return states


def on_device(positions, forces, self_blocks, cut_lists, pair_tiles):
    fibres = positions.shape[2]
    unknowns = 3 * NODES
    flat_forces = forces.reshape(unknowns, fibres)
    states = jnp.concatenate(
        [positions.reshape(unknowns, fibres), flat_forces, apply_blocks(self_blocks, flat_forces)],
        axis=0,
    ).T
    states = sectioned_move(states, cut_lists)
    self_velocity = states[:, 2 * unknowns :].T
    tiles_count = fibres // TILE
    near = rows_to_tiles(states[:, :unknowns], tiles_count) - 0.5
    push = rows_to_tiles(states[:, unknowns : 2 * unknowns], tiles_count)
    tiles = jnp.concatenate([near, push], axis=0).transpose(1, 0, 2)
    slab_count = lax.axis_size("slab")
    bis_count = lax.axis_size("bis")
    present = pair_tiles >= 0
    safe_ids = jnp.maximum(pair_tiles, 0)
    tile_local = safe_ids % tiles_count
    relative = (safe_ids // tiles_count // slab_count - lax.axis_index("bis")) % bis_count
    extended = with_halo(tiles, (("bis", 0),), tiles_count)
    lookup = jnp.where(
        relative == 0,
        tiles_count + tile_local,
        jnp.where(relative == 1, 2 * tiles_count + tile_local, tile_local),
    )
    empty = extended.shape[0]
    lookup = jnp.where(present, lookup, empty).astype(jnp.int32)
    near, push = extended[:, :3], extended[:, 3:]
    extended = jnp.concatenate(
        [
            extended,
            jnp.sum(near * near, axis=1, keepdims=True),
            -jnp.sum(near * push, axis=1, keepdims=True),
        ],
        axis=1,
    )
    extended = jnp.pad(extended, ((0, 8), (0, 0), (0, 0)))
    extended = jnp.concatenate([extended[tiles_count : 2 * tiles_count], extended], axis=0)
    stokes_velocity = stokes_tiles(extended, jnp.where(lookup >= 0, lookup + tiles_count, 0))
    return self_velocity.reshape(3, NODES, fibres) + from_tiles(stokes_velocity, tiles_count)


def solution(mesh):
    placed = (
        P(None, None, ("bis", "slab")),
        P(None, None, ("bis", "slab")),
        P(None, None, ("bis", "slab")),
        P(None, ("bis", "slab")),
        P(None, ("bis", "slab")),
    )
    return jax.shard_map(
        on_device,
        mesh=mesh,
        in_specs=placed,
        out_specs=P(None, None, ("bis", "slab")),
        check_vma=False,
    )
```

time: 345 us -> 180 us (0.52)
  other arithmetic: 216 us -> 17.2 us
  Pallas kernels: 0 us -> 78.2 us
  local copies, waits for them, and re-layouts: 57 us -> 22.1 us
  loops' own time: 11 us -> 0 us
    reduce_sum x32 -> x1, other arithmetic: 170 us -> 2.13 us  [on_device(): jnp.sum(near * near, axis=1, keepdims=True)]
    pallas_call x0 -> x1, Pallas kernels: none -> 78.2 us  [stokes_tiles(): pl.pallas_call(functools.partial(stokes_kernel, entries), out_shape=jax.S...]
    mul x16 -> x0, other arithmetic: 29.8 us -> none  [stokeslet(): dot_force * inverse3]
    dynamic_slice x48 -> x0, local copies, waits for them, and re-layouts: 23.3 us -> none  [the longest x16 11.8 us: stokes_block(): near = lax.dynamic_slice_in_dim(targets, first_tile, block_len, axis=1)]
    another operation x1 -> x0, loops' own time: 11 us -> none  [on_device(): lax.map(stokes_block, jnp.arange(tiles_count // block_len, dtype=jnp.int32))]
    gather x1 -> x0, local copies, waits for them, and re-layouts: 9.01 us -> none  [on_device(): jnp.take(extended, lookup.reshape(-1), axis=1)]
    sub x0 -> x3, local copies, waits for them, and re-layouts: none -> 3.94 us  [on_device(): near = rows_to_tiles(states[:, :unknowns], tiles_count) - 0.5]
    reshape x4 -> x2, local copies, waits for them, and re-layouts: 4.73 us -> 1.01 us  [rows_to_tiles(): rows.reshape(count, TILE, 3, NODES).transpose(2, 0, 1, 3)]
where the time goes in v1:
time: 180 us; the launch traced here: 178 us
  Pallas kernels  78.2 us (43%)
  waiting for transfers between devices  50.5 us (28%)
  local copies, waits for them, and re-layouts  22.1 us (12%)
  other arithmetic  17.2 us (10%)
  starting transfers between devices  9.79 us (5%)
    pallas_call x1, Pallas kernels, stokes_tiles(): pl.pallas_call(functools.partial(stokes_kernel, entries), out_shape=jax.S...  78.2 us
    ppermute x3, waiting for transfers between devices, swapped(): return lax.ppermute(block, axis, route)  32.8 us
    ppermute x1, waiting for transfers between devices, with_halo(): lax.ppermute(lax.slice_in_dim(block, 0, width, axis=dim), axis, backward)  17.7 us
    reduce_sum x1, other arithmetic, apply_blocks(): return jnp.sum(blocks.astype(jnp.float32) * flat_forces[None], axis=1)  8.92 us
    scatter x3, local copies, waits for them, and re-layouts, sectioned_move(): states = states.at[chosen].set(arrived)  6 us
    ppermute x3, starting transfers between devices, swapped(): return lax.ppermute(block, axis, route)  5.54 us
    sub x3, local copies, waits for them, and re-layouts, on_device(): near = rows_to_tiles(states[:, :unknowns], tiles_count) - 0.5  3.94 us
  transfers between devices with their start and end apart: 5, of which 4 were waited for; matrix products, arithmetic and copies ran while one was open for 1% of the time, Pallas kernels for 0%

profile of v1, /device:TPU:1, one launch (start us, length us, event | category | flops | bytes accessed | tf_op | source)
XLA Modules:
  0.0 178.1 jit_solution(13026046591066452119)
XLA Ops:
  0.0 0.8 fusion.8
  0.8 1.2 copy.24
  2.0 0.0 copy-start.1
  2.0 8.9 %multiply_reduce_fusion = f32[96,1024]{1,0:T(8,128)S(1)} fusion(bf16[96,96,1024]{2,1,0:T(8,128)(2,1)} %param.9, f32[96,1024]{1,0:T(8,128)} %bitcast.43), kind=kLoop, calls=%fused_computation.6 | loop fusion | flops 28213248 | bytes 19660800 | tf_op jit(solution)/shard_map/reduce_sum | solution.py:172
  11.0 0.2 copy.25
  11.2 0.0 copy-done.1
  11.2 0.2 copy.23
  11.4 0.0 copy-start.2
  11.4 0.6 maximum_bitcast_fusion
  12.0 1.0 gather_fusion
  13.0 0.1 broadcast_select_fusion.2
  13.1 3.2 %collective-permute-start = (f32[256,288]{1,0:T(8,128)S(1)}, f32[256,288]{1,0:T(8,128)S(1)}, u32[]{:S(2)}, u32[]{:S(2)}) collective-permute-start(f32[256,288]{1,0:T(8,128)S(1)} %broadcast_select_fusion.2), channel_id=1, source_target_pairs={{0,4},{4,0},{1,5},{5,1},{2,6},{6,2},{3,7},{7,3},{8,12},{12,8},{9,1... | collective-permute-start | bytes 884744 | tf_op jit(solution)/shard_map/ppermute | solution.py:144
  16.3 0.0 copy-done.2
  16.4 17.2 %collective-permute-done = f32[256,288]{1,0:T(8,128)S(1)} collective-permute-done((f32[256,288]{1,0:T(8,128)S(1)}, f32[256,288]{1,0:T(8,128)S(1)}, u32[]{:S(2)}, u32[]{:S(2)}) %collective-permute-start) | collective-permute-done | bytes 294944 | tf_op jit(solution)/shard_map/ppermute | solution.py:144
  33.6 2.0 %scatter_fusion = f32[1024,288]{1,0:T(8,128)S(1)} fusion(f32[1024,288]{1,0:T(8,128)S(1)} %maximum_bitcast_fusion, s32[256]{0:T(256)S(1)} %bitcast.54, f32[256,288]{1,0:T(8,128)S(1)} %collective-permute-done), kind=kCustom, calls=%fused_computation.3 | custom fusion | bytes 885760 | tf_op jit(solution)/shard_map/scatter | solution.py:180
  35.6 1.0 gather_fusion.1
  36.6 0.1 broadcast_select_fusion.1
  36.7 1.2 collective-permute-start.1
  37.9 8.2 %collective-permute-done.1 = f32[256,288]{1,0:T(8,128)S(1)} collective-permute-done((f32[256,288]{1,0:T(8,128)S(1)}, f32[256,288]{1,0:T(8,128)S(1)}, u32[]{:S(2)}, u32[]{:S(2)}) %collective-permute-start.1) | collective-permute-done | bytes 294944 | tf_op jit(solution)/shard_map/ppermute | solution.py:144
  46.1 2.0 %scatter_fusion.1 = f32[1024,288]{1,0:T(8,128)S(1)} fusion(f32[1024,288]{1,0:T(8,128)S(1)} %scatter_fusion, s32[256]{0:T(256)S(1)} %bitcast.53, f32[256,288]{1,0:T(8,128)S(1)} %collective-permute-done.1), kind=kCustom, calls=%fused_computation.4 | custom fusion | bytes 885760 | tf_op jit(solution)/shard_map/scatter | solution.py:180
  48.1 1.0 gather_fusion.2
  49.1 0.1 broadcast_select_fusion
  49.2 1.1 collective-permute-start.2
  50.3 7.4 %collective-permute-done.2 = f32[256,288]{1,0:T(8,128)S(1)} collective-permute-done((f32[256,288]{1,0:T(8,128)S(1)}, f32[256,288]{1,0:T(8,128)S(1)}, u32[]{:S(2)}, u32[]{:S(2)}) %collective-permute-start.2) | collective-permute-done | bytes 294944 | tf_op jit(solution)/shard_map/ppermute | solution.py:144
  57.8 2.0 %scatter_fusion.2 = f32[1024,288]{1,0:T(8,128)S(1)} fusion(f32[1024,288]{1,0:T(8,128)S(1)} %scatter_fusion.1, s32[256]{0:T(256)S(1)} %bitcast.52, f32[256,288]{1,0:T(8,128)S(1)} %collective-permute-done.2), kind=kCustom, calls=%fused_computation.5 | custom fusion | bytes 885760 | tf_op jit(solution)/shard_map/scatter | solution.py:180
  59.8 1.1 slice_add_fusion
  60.9 2.3 %sub.31 = f32[256,4,3,32]{3,2,1,0:T(4,128)S(1)} reshape(f32[1024,96]{1,0:T(8,128)} %get-tuple-element.8) | data formatting | bytes 786432 | tf_op jit(solution)/shard_map/sub | solution.py:195
  63.2 0.6 copy.27
  63.8 1.0 copy.29
  64.8 0.8 reshape.129
  65.6 0.0 copy-start
  65.6 0.0 copy-start.3
  65.6 0.6 copy.28
  66.3 0.2 copy.30
  66.5 0.1 copy-done
  66.6 0.2 maximum_bitcast_fusion.1
  66.9 0.2 copy.31
  67.0 3.1 %collective-permute-start.4 = (f32[256,6,128]{2,0,1:T(8,128)S(1)}, f32[256,6,128]{2,0,1:T(8,128)}, u32[]{:S(2)}, u32[]{:S(2)}) collective-permute-start(f32[256,6,128]{2,0,1:T(8,128)S(1)} %copy.31), channel_id=1, source_target_pairs={{8,0},{16,8},{24,16},{0,24},{9,1},{17,9},{25,17},{1,25},{10,2},{18... | collective-permute-start | bytes 2359304 | tf_op jit(solution)/shard_map/ppermute | solution.py:156
  70.1 1.1 collective-permute-start.3
  71.3 0.0 copy-done.3
  71.3 0.2 copy.26
  71.5 17.7 %collective-permute-done.4 = f32[256,6,128]{2,0,1:T(8,128)} collective-permute-done((f32[256,6,128]{2,0,1:T(8,128)S(1)}, f32[256,6,128]{2,0,1:T(8,128)}, u32[]{:S(2)}, u32[]{:S(2)}) %collective-permute-start.4) | collective-permute-done | bytes 786464 | tf_op jit(solution)/shard_map/ppermute | solution.py:156
  89.2 1.6 copy.34
  90.8 0.0 collective-permute-done.3
  90.8 1.6 copy.33
  92.4 0.3 pad_maximum_fusion
  92.7 2.1 %multiply_reduce_fusion.1 = (f32[768,128]{1,0:T(8,128)S(1)}, f32[768,128]{1,0:T(8,128)S(1)}) fusion(f32[768,6,128]{2,1,0:T(8,128)S(1)} %pad_maximum_fusion), kind=kLoop, calls=%fused_computation.14 | loop fusion | flops 983040 | bytes 3145728 | tf_op jit(solution)/shard_map/reduce_sum | solution.py:216
  94.9 1.0 pad_maximum_fusion.1
  96.0 0.1 slice.48
  96.0 1.7 select_maximum_fusion.ext
  97.8 78.2 %shard_map.55 = f32[3,256,128]{2,1,0:T(8,128)S(1)} custom-call(s32[4,256]{1,0:T(4,128)S(1)} %add_select_fusion.5.look, f32[1032,8,128]{2,1,0:T(8,128)S(1)} %select_maximum_fusion.ext), custom_call_target="tpu_custom_call" | custom-call | flops 400000000 | bytes 2000000 | tf_op jit(solution)/shard_map/pallas_call | solution.py:120
  175.9 0.2 copy.35
  176.1 0.7 copy.36
  176.8 0.4 copy.37
  177.3 0.8 add.78
  (12 shorter events, 0.1 us)
Async XLA Ops:
  2.0 9.1 %copy-start.1 = (f32[3,32,1024]{2,1,0:T(8,128)S(1)}, f32[3,32,1024]{2,1,0:T(8,128)}, u32[]{:S(2)}) copy-start(f32[3,32,1024]{2,1,0:T(8,128)} %param.7) | copy-start | bytes 1179652
  11.4 5.0 %copy-start.2 = (s32[3,256]{1,0:T(4,128)S(1)}, s32[3,256]{1,0:T(4,128)}, u32[]{:S(2)}) copy-start(s32[3,256]{1,0:T(4,128)} %param.10) | copy-start | bytes 9220
  13.1 20.5 %collective-permute-start = (f32[256,288]{1,0:T(8,128)S(1)}, f32[256,288]{1,0:T(8,128)S(1)}, u32[]{:S(2)}, u32[]{:S(2)}) collective-permute-start(f32[256,288]{1,0:T(8,128)S(1)} %broadcast_select_fusion.2), channel_id=1, source_target_pairs={{0,4},{4,0},{1,5},{5,1},{2,6},{6,2},{3,7},{7,3},{8,12},{12,8},{9,1... | collective-permute-start | bytes 884744 | tf_op jit(solution)/shard_map/ppermute | solution.py:144
  36.7 9.4 %collective-permute-start.1 = (f32[256,288]{1,0:T(8,128)S(1)}, f32[256,288]{1,0:T(8,128)S(1)}, u32[]{:S(2)}, u32[]{:S(2)}) collective-permute-start(f32[256,288]{1,0:T(8,128)S(1)} %broadcast_select_fusion.1), channel_id=1, source_target_pairs={{0,2},{2,0},{1,3},{3,1},{4,6},{6,4},{5,7},{7,5},{8,10},{10,8},{9,1... | collective-permute-start | bytes 884744 | tf_op jit(solution)/shard_map/ppermute | solution.py:144
  49.2 8.5 %collective-permute-start.2 = (f32[256,288]{1,0:T(8,128)S(1)}, f32[256,288]{1,0:T(8,128)S(1)}, u32[]{:S(2)}, u32[]{:S(2)}) collective-permute-start(f32[256,288]{1,0:T(8,128)S(1)} %broadcast_select_fusion), channel_id=1, source_target_pairs={{0,1},{1,0},{2,3},{3,2},{4,5},{5,4},{6,7},{7,6},{8,9},{9,8},{10,11... | collective-permute-start | bytes 884744 | tf_op jit(solution)/shard_map/ppermute | solution.py:144
  65.6 1.0 copy-start
  65.6 5.7 %copy-start.3 = (s32[4,256]{1,0:T(4,128)S(1)}, s32[4,256]{1,0:T(4,128)}, u32[]{:S(2)}) copy-start(s32[4,256]{1,0:T(4,128)} %param.11) | copy-start | bytes 12292
  67.0 22.2 %collective-permute-start.4 = (f32[256,6,128]{2,0,1:T(8,128)S(1)}, f32[256,6,128]{2,0,1:T(8,128)}, u32[]{:S(2)}, u32[]{:S(2)}) collective-permute-start(f32[256,6,128]{2,0,1:T(8,128)S(1)} %copy.31), channel_id=1, source_target_pairs={{8,0},{16,8},{24,16},{0,24},{9,1},{17,9},{25,17},{1,25},{10,2},{18... | collective-permute-start | bytes 2359304 | tf_op jit(solution)/shard_map/ppermute | solution.py:156
  70.1 20.7 %collective-permute-start.3 = (f32[256,6,128]{2,0,1:T(8,128)S(1)}, f32[256,6,128]{2,0,1:T(8,128)}, u32[]{:S(2)}, u32[]{:S(2)}) collective-permute-start(f32[256,6,128]{2,0,1:T(8,128)S(1)} %copy.31), channel_id=1, source_target_pairs={{0,8},{8,16},{16,24},{24,0},{1,9},{9,17},{17,25},{25,1},{2,10},{10... | collective-permute-start | bytes 2359304 | tf_op jit(solution)/shard_map/ppermute | solution.py:153

commit v2 on v1

--- a/solution.py
+++ b/solution.py
@@ -7,6 +7,37 @@
 
 NODES = 32
 TILE = 4
+REQ = 64
+
+
+def split3(x):
+    h1 = x.astype(jnp.bfloat16)
+    r = x - h1.astype(jnp.float32)
+    h2 = r.astype(jnp.bfloat16)
+    h3 = (r - h2.astype(jnp.float32)).astype(jnp.bfloat16)
+    return h1, h2, h3
+
+
+def dot_nn(a, b):
+    return lax.dot_general(a, b, (((1,), (0,)), ((), ())), preferred_element_type=jnp.float32)
+
+
+def dot_nt(a, b):
+    return lax.dot_general(a, b, (((1,), (1,)), ((), ())), preferred_element_type=jnp.float32)
+
+
+def pick(x, onehot):
+    h1, h2, h3 = split3(x)
+    return dot_nn(h1, onehot) + dot_nn(h2, onehot) + dot_nn(h3, onehot)
+
+
+def spread(x, onehot):
+    h1, h2, h3 = split3(x)
+    return dot_nt(h1, onehot) + dot_nt(h2, onehot) + dot_nt(h3, onehot)
+
+
+def flag(mask):
+    return jnp.where(mask, 1.0, 0.0).astype(jnp.bfloat16)
 
 
 blob_eps2 = 0.0025
@@ -43,7 +74,7 @@
     return jnp.concatenate([left, right], axis=1).astype(jnp.bfloat16)
 
 
-def stokes_kernel(entries, look, ext, out, packed, qp0, qp1, acc0, acc1):
+def stokes_kernel(entries, look, ext, own, final, out, packed, qp0, qp1, acc0, acc1):
     count = out.shape[1]
     total = ext.shape[0]
 
@@ -113,16 +144,31 @@
         sweep(g + 1, qp1, acc1)
         finish(g + 1, acc1)
 
-
-def stokes_tiles(ext, look):
+    fibres = final.shape[1]
+    back = flag(
+        lax.broadcasted_iota(jnp.int32, (fibres, fibres), 0)
+        == (lax.broadcasted_iota(jnp.int32, (fibres, fibres), 1) % TILE) * count
+        + lax.broadcasted_iota(jnp.int32, (fibres, fibres), 1) // TILE
+    )
+    for c in range(3):
+        turned = out[c].T
+        summed = own[c * NODES : (c + 1) * NODES] + jnp.concatenate(
+            [turned[t * NODES : (t + 1) * NODES] for t in range(TILE)], axis=1
+        )
+        final[c * NODES : (c + 1) * NODES] = pick(summed, back)
+
+
+def stokes_tiles(ext, look, own):
     entries, count = look.shape
     total = ext.shape[0]
     return pl.pallas_call(
         functools.partial(stokes_kernel, entries),
-        out_shape=jax.ShapeDtypeStruct((3, count, 128), jnp.float32),
-        in_specs=[pl.BlockSpec(memory_space=pltpu.SMEM), pl.BlockSpec(memory_space=pltpu.VMEM)],
+        out_shape=jax.ShapeDtypeStruct(own.shape, jnp.float32),
+        in_specs=[pl.BlockSpec(memory_space=pltpu.SMEM)]
+        + [pl.BlockSpec(memory_space=pltpu.VMEM)] * 2,
         out_specs=pl.BlockSpec(memory_space=pltpu.VMEM),
         scratch_shapes=[
+            pltpu.VMEM((3, count, 128), jnp.float32),
             pltpu.VMEM((total, 32, 128), jnp.bfloat16),
             pltpu.VMEM((256, entries * 128), jnp.float32),
             pltpu.VMEM((256, entries * 128), jnp.float32),
@@ -131,97 +177,244 @@
         ],
         compiler_params=pltpu.CompilerParams(vmem_limit_bytes=48 * 2**20),
         cost_estimate=pl.CostEstimate(flops=400_000_000, bytes_accessed=2_000_000, transcendentals=0),
-    )(look, ext)
-
-
-def swapped(block, axis, distance):
-    count = lax.axis_size(axis)
-    route = []
-    for low in range(count):
-        high = low | 1 << distance
-        if high != low and high < count:
-            route += [(low, high), (high, low)]
-    return lax.ppermute(block, axis, route)
-
-
-def with_halo(block, sides, width):
-    for axis, dim in sides:
-        count = lax.axis_size(axis)
-        forward = [(i, i + 1) for i in range(count - 1)]
-        forward.append((count - 1, 0))
-        backward = [(target, source) for source, target in forward]
-        low = lax.ppermute(
-            lax.slice_in_dim(block, block.shape[dim] - width, None, axis=dim), axis, forward
-        )
-        high = lax.ppermute(lax.slice_in_dim(block, 0, width, axis=dim), axis, backward)
-        block = jnp.concatenate([low, block, high], axis=dim)
-    return block
-
-
-def rows_to_tiles(rows, count):
-    return rows.reshape(count, TILE, 3, NODES).transpose(2, 0, 1, 3).reshape(3, count, TILE * NODES)
-
-
-def from_tiles(values, count):
-    return (
-        values.reshape(3, count, TILE, NODES).transpose(0, 3, 1, 2).reshape(3, NODES, count * TILE)
-    )
-
-
-def apply_blocks(blocks, flat_forces):
-    return jnp.sum(blocks.astype(jnp.float32) * flat_forces[None], axis=1)
-
-
-def sectioned_move(states, cut_lists):
-    levels = cut_lists.shape[0]
-    for section_no in range(levels):
-        chosen = cut_lists[section_no]
-        arrived = swapped(jnp.take(states, chosen, axis=0), "slab", levels - 1 - section_no)
-        states = states.at[chosen].set(arrived)
-    return states
+    )(look, ext, own)
+
+
+def exchange_kernel(
+    levels, pos, force, blocks, cuts, tile_ids, ext, own_out, look_out,
+    state, own, held, hots, perm, chunk, pf_out, pf_in, own_send, own_in,
+    code_out, code_in, halo_out, halo_in, chunk_sem, send_sem, recv_sem,
+):
+    fibres = pos.shape[1]
+    rows = pos.shape[0]
+    count = fibres // TILE
+    b, s = lax.axis_index("bis"), lax.axis_index("slab")
+    nb, ns = lax.axis_size("bis"), lax.axis_size("slab")
+    partners = []
+    for level in range(levels):
+        d = ns // 2 ** (level + 1)
+        partners.append(s + d - 2 * d * ((s // d) % 2))
+    right, left = (b + 1) % nb, (b + nb - 1) % nb
+
+    barrier = pltpu.get_barrier_semaphore()
+    for p in partners:
+        pl.semaphore_signal(barrier, inc=1, device_id={"slab": p}, device_id_type=pl.DeviceIdType.MESH)
+    for p in (right, left):
+        pl.semaphore_signal(barrier, inc=1, device_id={"bis": p}, device_id_type=pl.DeviceIdType.MESH)
+
+    depth = chunk.shape[0]
+    group = chunk.shape[1]
+    steps = rows // group
+
+    def fetch(k, slot):
+        return pltpu.make_async_copy(
+            blocks.at[pl.ds(k * group, group)], chunk.at[slot], chunk_sem.at[slot]
+        )
+
+    for k in range(depth - 1):
+        fetch(k, k).start()
+
+    def remote(src, dst, no, where):
+        return pltpu.make_async_remote_copy(
+            src_ref=src, dst_ref=dst, send_sem=send_sem.at[no], recv_sem=recv_sem.at[no],
+            device_id=where, device_id_type=pl.DeviceIdType.MESH,
+        )
+
+    slot_ids = lax.broadcasted_iota(jnp.int32, (fibres, cuts.shape[1]), 0)
+    first_hot = flag(slot_ids == cuts[0:1, :])
+    pf_out[0, 0:rows] = pick(pos[...], first_hot)
+    pf_out[0, rows:] = pick(force[...], first_hot)
+    pl.semaphore_wait(barrier, levels + 2)
+    pf = [remote(pf_out.at[l], pf_in.at[l], l, {"slab": partners[l]}) for l in range(levels)]
+    ov = [remote(own_send.at[l], own_in.at[l], levels + l, {"slab": partners[l]}) for l in range(levels)]
+    pf[0].start()
+
+    here = tile_ids[...]
+    local = here % count
+    rel = (here // count // ns - b + nb) % nb
+    tile_rows = lax.broadcasted_iota(jnp.int32, (count, here.shape[1]), 0)
+    earlier = flag(
+        lax.broadcasted_iota(jnp.int32, (count, count), 0)
+        < lax.broadcasted_iota(jnp.int32, (count, count), 1)
+    )
+    ones_row = jnp.ones((8, here.shape[1]), jnp.bfloat16)
+    slots = []
+    code = []
+    for no, side in ((0, 1), (1, nb - 1)):
+        asked = jnp.where((here >= 0) & (rel == side), local, -1)
+        hot = flag(tile_rows == asked[0:1])
+        named = flag(dot_nt(ones_row, hot) > 0.5)
+        rank = dot_nn(named, earlier)
+        slots.append(dot_nn(rank.astype(jnp.bfloat16), hot))
+        code_out[no] = jnp.where(named.astype(jnp.float32) > 0.5, rank, -1.0)
+        code.append(remote(
+            code_out.at[no], code_in.at[no], 2 * levels + no, {"bis": right if no == 0 else left}
+        ))
+        code[no].start()
+    look_out[...] = jnp.where(
+        here < 0,
+        count + 2 * REQ,
+        jnp.where(
+            rel == 0,
+            local,
+            jnp.where(
+                rel == 1,
+                count + slots[0].astype(jnp.int32),
+                count + REQ + slots[1].astype(jnp.int32),
+            ),
+        ),
+    )
+
+    source_ids = lax.broadcasted_iota(jnp.int32, (fibres, count), 0)
+    tile_cols = lax.broadcasted_iota(jnp.int32, (fibres, count), 1)
+    for t in range(TILE):
+        perm[:, t * count : (t + 1) * count] = flag(source_ids == tile_cols * TILE + t)
+    state[0:rows] = pick(pos[...], perm[...])
+    state[rows:] = pick(force[...], perm[...])
+    for l in range(levels):
+        cut = cuts[l : l + 1, :]
+        hots[l] = flag(slot_ids == (cut % TILE) * count + cut // TILE)
+
+    def self_step(k, carry):
+        slot = k % depth
+        fetch(k, slot).wait()
+
+        @pl.when(k + depth - 1 < steps)
+        def _():
+            fetch(k + depth - 1, (k + depth - 1) % depth).start()
+
+        made = []
+        for i in range(group):
+            parts = []
+            for lane in range(0, fibres, 256):
+                parts.append(jnp.sum(
+                    chunk[slot, i, :, lane : lane + 256].astype(jnp.float32)
+                    * force[:, lane : lane + 256], axis=0, keepdims=True))
+            made.append(jnp.concatenate(parts, axis=1))
+        own[pl.ds(pl.multiple_of(k * group, group), group)] = jnp.concatenate(made, axis=0)
+        return carry
+
+    lax.fori_loop(0, steps, self_step, 0)
+    own[...] = pick(own[...], perm[...])
+
+    def keep_mask(l):
+        return dot_nt(jnp.ones((8, cuts.shape[1]), jnp.bfloat16), hots[l])[0:1] > 0.5
+
+    def send_own(l):
+        own_send[l] = pick(own[...], hots[l])
+        ov[l].start()
+
+    def take_own(l):
+        ov[l].wait()
+        own[...] = jnp.where(keep_mask(l), spread(own_in[l], hots[l]), own[...])
+
+    def take_pf(l):
+        pf[l].wait()
+        state[...] = jnp.where(keep_mask(l), spread(pf_in[l], hots[l]), state[...])
+
+    send_own(0)
+    for l in range(levels):
+        take_pf(l)
+        if l + 1 < levels:
+            pf_out[l + 1] = pick(state[...], hots[l + 1])
+            pf[l + 1].start()
+        if l > 0:
+            take_own(l - 1)
+            send_own(l)
+
+    for c in range(6):
+        block = jnp.concatenate(
+            [state[c * NODES : (c + 1) * NODES, t * count : (t + 1) * count] for t in range(TILE)],
+            axis=0,
+        )
+        tile = block.T
+        held[:, c * 128 : (c + 1) * 128] = tile - 0.5 if c < 3 else tile
+
+    halo = []
+    rank_rows = lax.broadcasted_iota(jnp.int32, (REQ, count), 0).astype(jnp.float32)
+    for no in range(2):
+        code[no].wait()
+        chosen = flag(code_in[no, 0:1] == rank_rows)
+        halo_out[no] = dot_nn(chosen, split3(held[...])[0]) + dot_nn(
+            chosen, split3(held[...])[1]) + dot_nn(chosen, split3(held[...])[2])
+        halo.append(remote(
+            halo_out.at[no], halo_in.at[no], 2 * levels + 2 + no, {"bis": left if no == 0 else right}
+        ))
+        halo[no].start()
+
+    def lay(rows6, first, n):
+        parts = [rows6[:, c * 128 : (c + 1) * 128] for c in range(6)]
+        parts.append(sum(parts[i] * parts[i] for i in range(3)))
+        parts.append(-sum(parts[i] * parts[i + 3] for i in range(3)))
+        for c in range(8):
+            ext[pl.ds(first * 8 + c, n, stride=8), :] = parts[c]
+
+    lay(held[...], 0, count)
+    ext[(count + 2 * REQ) * 8 :] = jnp.zeros((64, 128), jnp.float32)
+    for no in range(2):
+        halo[no].wait()
+        lay(halo_in[no], count + no * REQ, REQ)
+    take_own(levels - 1)
+    own_out[...] = own[...]
+
+
+def exchange(pos, force, blocks, cuts, tile_ids):
+    rows, fibres = pos.shape
+    levels, k = cuts.shape
+    count = fibres // TILE
+    total = count + 2 * REQ + 8
+    vmem = pl.BlockSpec(memory_space=pltpu.VMEM)
+    f32 = jnp.float32
+    return pl.pallas_call(
+        functools.partial(exchange_kernel, levels),
+        out_shape=(
+            jax.ShapeDtypeStruct((total * 8, 128), f32),
+            jax.ShapeDtypeStruct((rows, fibres), f32),
+            jax.ShapeDtypeStruct(tile_ids.shape, jnp.int32),
+        ),
+        in_specs=[vmem, vmem, pl.BlockSpec(memory_space=pl.ANY), vmem, vmem],
+        out_specs=(vmem, vmem, vmem),
+        scratch_shapes=[
+            pltpu.VMEM((2 * rows, fibres), f32),
+            pltpu.VMEM((rows, fibres), f32),
+            pltpu.VMEM((count, 6 * 128), f32),
+            pltpu.VMEM((levels, fibres, k), jnp.bfloat16),
+            pltpu.VMEM((fibres, fibres), jnp.bfloat16),
+            pltpu.VMEM((3, 8, rows, fibres), jnp.bfloat16),
+            pltpu.VMEM((levels, 2 * rows, k), f32),
+            pltpu.VMEM((levels, 2 * rows, k), f32),
+            pltpu.VMEM((levels, rows, k), f32),
+            pltpu.VMEM((levels, rows, k), f32),
+            pltpu.VMEM((2, 8, count), f32),
+            pltpu.VMEM((2, 8, count), f32),
+            pltpu.VMEM((2, REQ, 6 * 128), f32),
+            pltpu.VMEM((2, REQ, 6 * 128), f32),
+            pltpu.SemaphoreType.DMA((3,)),
+            pltpu.SemaphoreType.DMA((2 * levels + 4,)),
+            pltpu.SemaphoreType.DMA((2 * levels + 4,)),
+        ],
+        compiler_params=pltpu.CompilerParams(
+            collective_id=0, has_side_effects=True, vmem_limit_bytes=56 * 2**20
+        ),
+        cost_estimate=pl.CostEstimate(
+            flops=400_000_000, bytes_accessed=20_000_000, transcendentals=0
+        ),
+    )(pos, force, blocks, cuts, tile_ids)
 
 
 def on_device(positions, forces, self_blocks, cut_lists, pair_tiles):
     fibres = positions.shape[2]
     unknowns = 3 * NODES
-    flat_forces = forces.reshape(unknowns, fibres)
-    states = jnp.concatenate(
-        [positions.reshape(unknowns, fibres), flat_forces, apply_blocks(self_blocks, flat_forces)],
-        axis=0,
-    ).T
-    states = sectioned_move(states, cut_lists)
-    self_velocity = states[:, 2 * unknowns :].T
-    tiles_count = fibres // TILE
-    near = rows_to_tiles(states[:, :unknowns], tiles_count) - 0.5
-    push = rows_to_tiles(states[:, unknowns : 2 * unknowns], tiles_count)
-    tiles = jnp.concatenate([near, push], axis=0).transpose(1, 0, 2)
-    slab_count = lax.axis_size("slab")
-    bis_count = lax.axis_size("bis")
-    present = pair_tiles >= 0
-    safe_ids = jnp.maximum(pair_tiles, 0)
-    tile_local = safe_ids % tiles_count
-    relative = (safe_ids // tiles_count // slab_count - lax.axis_index("bis")) % bis_count
-    extended = with_halo(tiles, (("bis", 0),), tiles_count)
-    lookup = jnp.where(
-        relative == 0,
-        tiles_count + tile_local,
-        jnp.where(relative == 1, 2 * tiles_count + tile_local, tile_local),
-    )
-    empty = extended.shape[0]
-    lookup = jnp.where(present, lookup, empty).astype(jnp.int32)
-    near, push = extended[:, :3], extended[:, 3:]
-    extended = jnp.concatenate(
-        [
-            extended,
-            jnp.sum(near * near, axis=1, keepdims=True),
-            -jnp.sum(near * push, axis=1, keepdims=True),
-        ],
-        axis=1,
-    )
-    extended = jnp.pad(extended, ((0, 8), (0, 0), (0, 0)))
-    extended = jnp.concatenate([extended[tiles_count : 2 * tiles_count], extended], axis=0)
-    stokes_velocity = stokes_tiles(extended, jnp.where(lookup >= 0, lookup + tiles_count, 0))
-    return self_velocity.reshape(3, NODES, fibres) + from_tiles(stokes_velocity, tiles_count)
+    count = fibres // TILE
+    ids = jnp.broadcast_to(pair_tiles.reshape(1, -1), (8, pair_tiles.size))
+    ext, own, look = exchange(
+        positions.reshape(unknowns, fibres), forces.reshape(unknowns, fibres),
+        self_blocks, cut_lists, ids,
+    )
+    moved = stokes_tiles(
+        ext.reshape(-1, 8, 128), look[0].reshape(pair_tiles.shape), own
+    )
+    return moved.reshape(3, NODES, fibres)
 
 
 def solution(mesh):

time: 180 us -> 132 us (0.73); the launches traced: 178 us -> 132 us
  waiting for transfers between devices: 50.5 us -> 0 us
  Pallas kernels: 78.2 us -> 127 us
  local copies, waits for them, and re-layouts: 22.1 us -> 4.49 us
  other arithmetic: 17.2 us -> 0 us
  starting transfers between devices: 9.79 us -> 0 us
    ppermute x5 -> x0, waiting for transfers between devices: 50.5 us -> none  [the longest x3 32.8 us: swapped(): return lax.ppermute(block, axis, route)]
    pallas_call x0 -> x1, Pallas kernels: none -> 46.1 us  [exchange(): pl.pallas_call(functools.partial(exchange_kernel, levels), out_shape=(jax...]
    reduce_sum x2 -> x0, other arithmetic: 11 us -> none  [the longest x1 8.92 us: apply_blocks(): return jnp.sum(blocks.astype(jnp.float32) * flat_forces[None], axis=1)]
    ppermute x5 -> x0, starting transfers between devices: 9.79 us -> none  [the longest x3 5.54 us: swapped(): return lax.ppermute(block, axis, route)]
    scatter x3 -> x0, local copies, waits for them, and re-layouts: 6 us -> none  [sectioned_move(): states = states.at[chosen].set(arrived)]
    sub x3 -> x0, local copies, waits for them, and re-layouts: 3.94 us -> none  [on_device(): near = rows_to_tiles(states[:, :unknowns], tiles_count) - 0.5]
    ppermute x2 -> x0, local copies, waits for them, and re-layouts: 3.22 us -> none  [the longest x1 1.61 us: with_halo(): lax.ppermute(lax.slice_in_dim(block, block.shape[dim] - width, None, axis...]
    pallas_call x1, Pallas kernels: 78.2 us -> 81.3 us  [stokes_tiles(): pl.pallas_call(functools.partial(stokes_kernel, entries), out_shape=jax.S...]
  transfers between devices with their start and end apart: 5 -> 0, of which waited for: 4 -> 0; matrix products, arithmetic and copies ran while one was open for 1% -> 0% of each run, Pallas kernels for 0% -> 0%
where the time goes in v2:
time: 132 us
  Pallas kernels  127 us (96%)
  local copies, waits for them, and re-layouts  4.49 us (3%)
    pallas_call x1, Pallas kernels, stokes_tiles(): pl.pallas_call(functools.partial(stokes_kernel, entries), out_shape=jax.S...  81.3 us
    pallas_call x1, Pallas kernels, exchange(): pl.pallas_call(functools.partial(exchange_kernel, levels), out_shape=(jax...  46.1 us
    unnamed x5, local copies, waits for them, and re-layouts  3.1 us

profile of v2, /device:TPU:1, one launch (start us, length us, event | category | flops | bytes accessed | tf_op | source)
XLA Modules:
  0.0 131.9 jit_solution(9881950265920071274)
XLA Ops:
  0.0 0.7 copy.6
  0.7 0.6 broadcast_in_dim.8.tile_ids
  1.3 46.1 %shard_map.55 = (f32[3136,128]{1,0:T(8,128)}, f32[96,1024]{1,0:T(8,128)}, s32[8,1024]{1,0:T(8,128)}) custom-call(f32[96,1024]{1,0:T(8,128)} %bitcast.7, f32[96,1024]{1,0:T(8,128)} %bitcast.8, bf16[96,96,1024]{2,1,0:T(8,128)(2,1)} %blocks.1, s32[3,256]{1,0:T(4,128)} %cuts.1, s32[8,1024]{1,0:T(8,128)} %broadcast_in_dim.8.tile_ids), custom_call_target="tpu_custom_call" | custom-call | flops 400000000 | bytes 20000000 | tf_op jit(solution)/shard_map/pallas_call | solution.py:368
  47.4 0.8 slice_reduce_fusion
  48.2 0.0 copy-start
  48.2 1.4 %copy-done = f32[3136,128]{1,0:T(8,128)S(1)} copy-done((f32[3136,128]{1,0:T(8,128)S(1)}, f32[3136,128]{1,0:T(8,128)}, u32[]{:S(2)}) %copy-start) | copy-done | bytes 1605656
  49.6 0.0 copy-start.1
  49.6 1.0 copy-done.1
  50.6 81.3 %shard_map.56 = f32[96,1024]{1,0:T(8,128)} custom-call(s32[4,256]{1,0:T(4,128)S(1)} %reshape_squeeze.3.look, f32[392,8,128]{2,1,0:T(8,128)S(1)} %bitcast.6, f32[96,1024]{1,0:T(8,128)S(1)} %copy-done.1), custom_call_target="tpu_custom_call" | custom-call | flops 400000000 | bytes 2000000 | tf_op jit(solution)/shard_map/pallas_call | solution.py:164
  (1 shorter events, 0.0 us)
Async XLA Ops:
  48.2 1.4 %copy-start = (f32[3136,128]{1,0:T(8,128)S(1)}, f32[3136,128]{1,0:T(8,128)}, u32[]{:S(2)}) copy-start(f32[3136,128]{1,0:T(8,128)} %get-tuple-element.9) | copy-start | bytes 4816900
  49.6 1.0 copy-start.1

commit v3 on v2

--- a/solution.py
+++ b/solution.py
@@ -115,21 +115,14 @@
                 part = [w * fs[n][i] - s * ys[n][i] for i in range(3)] + [s]
                 tot = part if tot is None else [a + b for a, b in zip(tot, part)]
             for i in range(4):
-                high = tot[i].astype(jnp.bfloat16).astype(jnp.float32)
                 acc[i * 128 + c * 8 : i * 128 + c * 8 + 8, 0:128] = tot[i]
 
     def finish(g, acc):
-        a = acc[...]
-        high = a.astype(jnp.bfloat16)
-        low = (a - high.astype(jnp.float32)).astype(jnp.bfloat16)
-        sums = lax.dot_general(
-            jnp.ones((8, 256), jnp.bfloat16), jnp.concatenate([high, low], axis=1),
-            (((1,), (1,)), ((), ())), preferred_element_type=jnp.float32,
-        )
+        sums = [jnp.sum(acc[i*128:i*128+128].T, axis=0, keepdims=True) for i in range(4)]
         t = ext[g]
         for i in range(3):
             out[i, pl.ds(g, 1)] = stokes_scale * (
-                sums[0:1, i * 128 : i * 128 + 128] + t[i : i + 1] * sums[0:1, 384:512]
+                sums[i] + t[i : i + 1] * sums[3]
             )
 
     products(0, qp0)
@@ -137,12 +130,14 @@
     @pl.loop(0, count // 2)
     def _(h):
         g = h * 2
+        finish(jnp.maximum(g - 1, 0), acc1)
         products(g + 1, qp1)
         sweep(g, qp0, acc0)
+        finish(g, acc0)
         products(jnp.minimum(g + 2, count - 1), qp0)
-        finish(g, acc0)
         sweep(g + 1, qp1, acc1)
-        finish(g + 1, acc1)
+
+    finish(count - 1, acc1)
 
     fibres = final.shape[1]
     back = flag(

time: 132 us -> 110 us (0.83)
  Pallas kernels: 127 us -> 105 us
    pallas_call x1, Pallas kernels: 81.3 us -> 58.6 us  [stokes_tiles(): pl.pallas_call(functools.partial(stokes_kernel, entries), out_shape=jax.S...]
where the time goes in v3:
time: 110 us; the launch traced here: 109 us
  Pallas kernels  105 us (95%)
  local copies, waits for them, and re-layouts  4.49 us (4%)
    pallas_call x1, Pallas kernels, stokes_tiles(): pl.pallas_call(functools.partial(stokes_kernel, entries), out_shape=jax.S...  58.6 us
    pallas_call x1, Pallas kernels, exchange(): pl.pallas_call(functools.partial(exchange_kernel, levels), out_shape=(jax...  46.1 us
    unnamed x5, local copies, waits for them, and re-layouts  3.1 us

profile of v3, /device:TPU:1, one launch (start us, length us, event | category | flops | bytes accessed | tf_op | source)
XLA Modules:
  0.0 109.3 jit_solution(12467767468405175699)
XLA Ops:
  0.0 0.7 copy.6
  0.7 0.6 broadcast_in_dim.8.tile_ids
  1.3 46.1 %shard_map.55 = (f32[3136,128]{1,0:T(8,128)}, f32[96,1024]{1,0:T(8,128)}, s32[8,1024]{1,0:T(8,128)}) custom-call(f32[96,1024]{1,0:T(8,128)} %bitcast.7, f32[96,1024]{1,0:T(8,128)} %bitcast.8, bf16[96,96,1024]{2,1,0:T(8,128)(2,1)} %blocks.1, s32[3,256]{1,0:T(4,128)} %cuts.1, s32[8,1024]{1,0:T(8,128)} %broadcast_in_dim.8.tile_ids), custom_call_target="tpu_custom_call" | custom-call | flops 400000000 | bytes 20000000 | tf_op jit(solution)/shard_map/pallas_call | solution.py:363
  47.4 0.8 slice_reduce_fusion
  48.2 0.0 copy-start
  48.2 1.4 %copy-done = f32[3136,128]{1,0:T(8,128)S(1)} copy-done((f32[3136,128]{1,0:T(8,128)S(1)}, f32[3136,128]{1,0:T(8,128)}, u32[]{:S(2)}) %copy-start) | copy-done | bytes 1605656
  49.6 0.0 copy-start.1
  49.6 1.0 copy-done.1
  50.6 58.6 %shard_map.56 = f32[96,1024]{1,0:T(8,128)} custom-call(s32[4,256]{1,0:T(4,128)S(1)} %reshape_squeeze.3.look, f32[392,8,128]{2,1,0:T(8,128)S(1)} %bitcast.6, f32[96,1024]{1,0:T(8,128)S(1)} %copy-done.1), custom_call_target="tpu_custom_call" | custom-call | flops 400000000 | bytes 2000000 | tf_op jit(solution)/shard_map/pallas_call | solution.py:159
  (1 shorter events, 0.0 us)
Async XLA Ops:
  48.2 1.4 %copy-start = (f32[3136,128]{1,0:T(8,128)S(1)}, f32[3136,128]{1,0:T(8,128)}, u32[]{:S(2)}) copy-start(f32[3136,128]{1,0:T(8,128)} %get-tuple-element.9) | copy-start | bytes 4816900
  49.6 1.0 copy-start.1

commit v4 on v3

--- a/solution.py
+++ b/solution.py
@@ -326,12 +326,16 @@
         held[:, c * 128 : (c + 1) * 128] = tile - 0.5 if c < 3 else tile
 
     halo = []
+    tile_parts = split3(held[...])
     rank_rows = lax.broadcasted_iota(jnp.int32, (REQ, count), 0).astype(jnp.float32)
     for no in range(2):
         code[no].wait()
         chosen = flag(code_in[no, 0:1] == rank_rows)
-        halo_out[no] = dot_nn(chosen, split3(held[...])[0]) + dot_nn(
-            chosen, split3(held[...])[1]) + dot_nn(chosen, split3(held[...])[2])
+        halo_out[no] = (
+            dot_nn(chosen, tile_parts[0])
+            + dot_nn(chosen, tile_parts[1])
+            + dot_nn(chosen, tile_parts[2])
+        )
         halo.append(remote(
             halo_out.at[no], halo_in.at[no], 2 * levels + 2 + no, {"bis": left if no == 0 else right}
         ))

time: 110 us -> 110 us (level)
  no operation moved by 1% of the time
where the time goes in v4:
time: 110 us; the launch traced here: 109 us
  Pallas kernels  105 us (95%)
  local copies, waits for them, and re-layouts  4.49 us (4%)
    pallas_call x1, Pallas kernels, stokes_tiles(): pl.pallas_call(functools.partial(stokes_kernel, entries), out_shape=jax.S...  58.6 us
    pallas_call x1, Pallas kernels, exchange(): pl.pallas_call(functools.partial(exchange_kernel, levels), out_shape=(jax...  46.1 us
    unnamed x5, local copies, waits for them, and re-layouts  3.1 us

profile of v4, /device:TPU:1, one launch (start us, length us, event | category | flops | bytes accessed | tf_op | source)
XLA Modules:
  0.0 109.3 jit_solution(9616607945379275255)
XLA Ops:
  0.0 0.7 copy.6
  0.7 0.6 broadcast_in_dim.8.tile_ids
  1.3 46.1 %shard_map.55 = (f32[3136,128]{1,0:T(8,128)}, f32[96,1024]{1,0:T(8,128)}, s32[8,1024]{1,0:T(8,128)}) custom-call(f32[96,1024]{1,0:T(8,128)} %bitcast.7, f32[96,1024]{1,0:T(8,128)} %bitcast.8, bf16[96,96,1024]{2,1,0:T(8,128)(2,1)} %blocks.1, s32[3,256]{1,0:T(4,128)} %cuts.1, s32[8,1024]{1,0:T(8,128)} %broadcast_in_dim.8.tile_ids), custom_call_target="tpu_custom_call" | custom-call | flops 400000000 | bytes 20000000 | tf_op jit(solution)/shard_map/pallas_call | solution.py:367
  47.4 0.8 slice_reduce_fusion
  48.2 0.0 copy-start
  48.2 1.4 %copy-done = f32[3136,128]{1,0:T(8,128)S(1)} copy-done((f32[3136,128]{1,0:T(8,128)S(1)}, f32[3136,128]{1,0:T(8,128)}, u32[]{:S(2)}) %copy-start) | copy-done | bytes 1605656
  49.6 0.0 copy-start.1
  49.6 1.0 copy-done.1
  50.6 58.6 %shard_map.56 = f32[96,1024]{1,0:T(8,128)} custom-call(s32[4,256]{1,0:T(4,128)S(1)} %reshape_squeeze.3.look, f32[392,8,128]{2,1,0:T(8,128)S(1)} %bitcast.6, f32[96,1024]{1,0:T(8,128)S(1)} %copy-done.1), custom_call_target="tpu_custom_call" | custom-call | flops 400000000 | bytes 2000000 | tf_op jit(solution)/shard_map/pallas_call | solution.py:159
  (1 shorter events, 0.0 us)
Async XLA Ops:
  48.2 1.4 %copy-start = (f32[3136,128]{1,0:T(8,128)S(1)}, f32[3136,128]{1,0:T(8,128)}, u32[]{:S(2)}) copy-start(f32[3136,128]{1,0:T(8,128)} %get-tuple-element.9) | copy-start | bytes 4816900
  49.6 1.0 copy-start.1
